TPU v7x, 32 devices: a whole 2x2x4 slice. The times are simulated.
32 devices in a mesh: sy: 4 (over z), sx: 4 (over y, core), tp: 2 (over x).
Axes of the slice: x: 2, y: 2, z: 4, core: 2. Of those that a mesh axis runs over, the one named last changes fastest.
Arguments:
- features: bfloat16 [96, 64, 1408], P('sy', 'sx', 'tp'), may hold values from -6 to 6
- depth_kernel: float32 [7, 7, 1408], P(None, None, 'tp'), may hold values from -0.875 to 0.875
- depth_bias: float32 [1408], P('tp'), may hold values from -1 to 1
- norm_gain: float32 [1408], replicated, may hold values from 0.1 to 1.9
- norm_bias: float32 [1408], replicated, may hold values from -3 to 3
- up_weight: bfloat16 [1408, 5632], P(None, 'tp'), may hold values from -0.15625 to 0.15625
- up_bias: float32 [5632], P('tp'), may hold values from -3 to 3
- response_gain: float32 [5632], P('tp'), may hold values from -4 to 4
- response_shift: float32 [5632], P('tp'), may hold values from -3 to 3
- down_weight: bfloat16 [5632, 1408], P('tp', ('sy', 'sx')), may hold values from -0.078125 to 0.078125
- down_bias: float32 [1408], P('tp'), may hold values from -3 to 3
- tissue: int32 [12, 8], P('sy', 'sx'), may hold values from 0 to 1, as said below
- cotangent: bfloat16 [96, 64, 1408], P('sy', 'sx', 'tp'), may hold values from -6 to 6
Outputs:
- block_out: bfloat16 [96, 64, 1408], P('sy', 'sx', 'tp')
- feature_grad: bfloat16 [96, 64, 1408], P('sy', 'sx', 'tp')
Inputs may be any that keep to these rules, and one draw needn't show every extreme that they name: Each device's block of 3 x 2 tiles holds 1 to 4 tissue tiles; some device's block holds exactly 4.
All inputs are finite; a program needn't handle non-finite values.
Results may differ from a plain program's by a relative error of at most 0.0049.
The roundings to bfloat16 on the way count: a program that leaves them out, or rounds other values in their place, can miss the bound.
Values may be sent and summed in bfloat16 or wider, within the bound.
A program may use at most 128 MiB of HBM per device.

v0:
```python
import jax
import jax.numpy as jnp
from jax import lax
from jax.sharding import PartitionSpec as P

KERNEL = 7
TILE = 8
root_half = 0.7071067811865476
root_two_pi_inv = 0.3989422804014327


def extended(block, sides, width):
    for axis, dim in sides:
        count = lax.axis_size(axis)
        forward = [(i, i + 1) for i in range(count - 1)]
        backward = [(target, source) for source, target in forward]
        low = lax.ppermute(
            lax.slice_in_dim(block, block.shape[dim] - width, None, axis=dim), axis, forward
        )
        high = lax.ppermute(lax.slice_in_dim(block, 0, width, axis=dim), axis, backward)
        block = jnp.concatenate([low, block, high], axis=dim)
    return block


def gelu_value(values):
    return 0.5 * values * (1.0 + jax.scipy.special.erf(values * root_half))


def gelu_slope(values):
    return (
        0.5 * (1.0 + jax.scipy.special.erf(values * root_half))
        + values * jnp.exp(-0.5 * values * values) * root_two_pi_inv
    )


def depthwise(padded, kernel, rows_out, cols_out, flipped):
    summed = jnp.zeros((rows_out, cols_out, kernel.shape[2]), jnp.float32)
    last_tap = KERNEL - 1
    for row_tap in range(KERNEL):
        for col_tap in range(KERNEL):
            row_start = last_tap - row_tap if flipped else row_tap
            col_start = last_tap - col_tap if flipped else col_tap
            window = padded[row_start : row_start + rows_out, col_start : col_start + cols_out]
            summed = summed + window.astype(jnp.float32) * kernel[row_tap, col_tap]
    return summed


MOST = 4


def extend(image):
    return extended(image, (("sy", 0), ("sx", 1)), KERNEL // 2)


def swapped(array):
    count = lax.axis_size("tp")
    return lax.ppermute(array, "tp", [(i, count - 1 - i) for i in range(count)])


def over_pixels(vector):
    return lax.psum(vector, ("sy", "sx"))


def conv_tiles(windows, kernel):
    summed = jnp.zeros((windows.shape[0], TILE, TILE, windows.shape[3]), jnp.float32)
    for row_tap in range(KERNEL):
        for col_tap in range(KERNEL):
            window = windows[:, row_tap : row_tap + TILE, col_tap : col_tap + TILE]
            summed = summed + window.astype(jnp.float32) * kernel[row_tap, col_tap]
    return summed


def shards(
    features,
    depth_kernel,
    depth_bias,
    norm_gain,
    norm_bias,
    up_weight,
    up_bias,
    response_gain,
    response_shift,
    down_weight,
    down_bias,
    tissue,
    cotangent,
):
    image_rows, image_cols, local_channels = features.shape
    tiles_y, tiles_x = tissue.shape
    tiles = tiles_y * tiles_x
    channels = up_weight.shape[0]
    hidden_total = up_weight.shape[1] * lax.axis_size("tp")
    tp_index = lax.axis_index("tp")
    first = tp_index == 0
    channel_start = tp_index * local_channels
    other_start = (1 - tp_index) * local_channels
    contract_last = (((1,), (1,)), ((), ()))
    pixels = MOST * TILE * TILE
    down_t = lax.all_gather(down_weight.T, ("sy", "sx"), axis=0, tiled=True)
    flags = tissue.reshape(-1)
    tile_ids = jnp.arange(tiles, dtype=jnp.int32)
    earlier = (tile_ids[None, :] < tile_ids[:, None]).astype(jnp.int32)
    ahead = jnp.sum(earlier * flags[None, :], axis=1)
    slot_of = jnp.where(flags > 0, ahead, jnp.sum(flags) + tile_ids - ahead)
    chosen = [jnp.sum(jnp.where(slot_of == s, tile_ids, 0)) for s in range(MOST)]
    slot_mask = jnp.stack([jnp.sum(jnp.where(slot_of == s, flags, 0)) for s in range(MOST)])
    mask_rows = jnp.repeat(slot_mask, TILE * TILE).astype(jnp.float32)

    def windows_of(image, side):
        return jnp.stack(
            [
                lax.dynamic_slice(
                    image,
                    (t // tiles_x * TILE, t % tiles_x * TILE, 0),
                    (side, side, image.shape[2]),
                )
                for t in chosen
            ]
        )

    def spread_out(rows_array):
        held = rows_array.reshape(MOST, TILE, TILE, rows_array.shape[1])
        held = jnp.concatenate([held, jnp.zeros_like(held[:1])], axis=0)
        slots = jnp.minimum(slot_of, MOST)
        rows = []
        for ty in range(tiles_y):
            row = [
                lax.dynamic_index_in_dim(held, slots[ty * tiles_x + tx], 0, keepdims=False)
                for tx in range(tiles_x)
            ]
            rows.append(jnp.concatenate(row, axis=1))
        return jnp.concatenate(rows, axis=0)

    def both_halves(own):
        other = swapped(own)
        return jnp.where(
            first, jnp.concatenate([own, other], axis=1), jnp.concatenate([other, own], axis=1)
        )

    cot_tiles = windows_of(cotangent, TILE).reshape(pixels, local_channels)
    masked_cot = (cot_tiles.astype(jnp.float32) * mask_rows[:, None]).astype(jnp.bfloat16)
    cot_wide = both_halves(masked_cot)
    convolved = conv_tiles(windows_of(extend(features), TILE + KERNEL - 1), depth_kernel)
    convolved = (convolved + depth_bias).astype(jnp.bfloat16).reshape(pixels, local_channels)
    gathered = both_halves(convolved).astype(jnp.float32)
    centre = jnp.mean(gathered, axis=1, keepdims=True)
    spread = jnp.mean(jnp.square(gathered - centre), axis=1, keepdims=True)
    inv_scale = lax.rsqrt(spread + 1e-06)
    standard = (gathered - centre) * inv_scale
    normed = (standard * norm_gain + norm_bias).astype(jnp.bfloat16)
    preact = jnp.dot(normed, up_weight, preferred_element_type=jnp.float32) + up_bias
    hidden = gelu_value(preact).astype(jnp.bfloat16)
    hidden_wide = hidden.astype(jnp.float32)
    squares = over_pixels(jnp.sum(mask_rows[:, None] * hidden_wide * hidden_wide, axis=0))
    column_norms = jnp.sqrt(squares)
    norms_here = jnp.full((8, 128), jnp.sum(column_norms))
    norm_level = (norms_here + swapped(norms_here))[0, 0] / hidden_total + 1e-06
    norm_ratio = column_norms / norm_level
    back_hidden = jnp.dot(cot_wide, down_t, preferred_element_type=jnp.float32)
    products = over_pixels(jnp.sum(back_hidden * hidden_wide, axis=0))
    response = (response_gain * hidden_wide * norm_ratio + response_shift + hidden_wide).astype(
        jnp.bfloat16
    )
    partial_out = lax.dot_general(
        response, down_t, contract_last, preferred_element_type=jnp.float32
    )
    sent_out = lax.dynamic_slice_in_dim(partial_out, other_start, local_channels, 1)
    kept_out = lax.dynamic_slice_in_dim(partial_out, channel_start, local_channels, 1)
    branch = kept_out + swapped(sent_out.astype(jnp.bfloat16)).astype(jnp.float32)
    ratio_grad = response_gain * products
    dots_here = jnp.full((8, 128), jnp.sum(ratio_grad * column_norms))
    dots = (dots_here + swapped(dots_here))[0, 0]
    norms_grad = ratio_grad / norm_level - dots / (hidden_total * norm_level * norm_level)
    hidden_grad = (
        back_hidden * (response_gain * norm_ratio + 1.0)
        + norms_grad * mask_rows[:, None] * hidden_wide / column_norms
    )
    preact_grad = (hidden_grad * gelu_slope(preact)).astype(jnp.bfloat16)
    grad_terms = lax.dot_general(
        preact_grad, up_weight, contract_last, preferred_element_type=jnp.float32
    )
    scaled_terms = grad_terms * norm_gain
    sums_here = jnp.stack([jnp.sum(scaled_terms, axis=1), jnp.sum(scaled_terms * standard, axis=1)])
    sums = sums_here + swapped(sums_here)
    sent_grad = lax.dynamic_slice_in_dim(scaled_terms, other_start, local_channels, 1)
    kept_grad = lax.dynamic_slice_in_dim(scaled_terms, channel_start, local_channels, 1)
    own_standard = lax.dynamic_slice_in_dim(standard, channel_start, local_channels, 1)
    scaled = kept_grad + swapped(sent_grad.astype(jnp.bfloat16)).astype(jnp.float32)
    convolved_grad = inv_scale * (
        scaled - (sums[0] / channels)[:, None] - own_standard * (sums[1] / channels)[:, None]
    )
    grad_image = spread_out(convolved_grad.astype(jnp.bfloat16))
    feature_grad = (
        cotangent.astype(jnp.float32)
        + depthwise(extend(grad_image), depth_kernel, image_rows, image_cols, True)
    ).astype(jnp.bfloat16)
    addend = spread_out(mask_rows[:, None] * (branch + down_bias))
    block_out = (features.astype(jnp.float32) + addend).astype(jnp.bfloat16)
    return (block_out, feature_grad)


def solution(mesh):
    placed = (
        P("sy", "sx", "tp"),
        P(None, None, "tp"),
        P("tp"),
        P(),
        P(),
        P(None, "tp"),
        P("tp"),
        P("tp"),
        P("tp"),
        P("tp", ("sy", "sx")),
        P("tp"),
        P("sy", "sx"),
        P("sy", "sx", "tp"),
    )
    return jax.shard_map(
        shards,
        mesh=mesh,
        in_specs=placed,
        out_specs=(P("sy", "sx", "tp"), P("sy", "sx", "tp")),
        check_vma=False,
    )
```

profile of v0, /device:TPU:12, one launch (start us, length us, event | category | flops | bytes accessed | tf_op | source)
XLA Modules:
  0.0 235.3 jit_solution(2763965542860036640)
XLA Ops:
  7.2 0.7 all-gather.2.cloned.1.call-update
  7.9 1.0 fusion.105
  8.9 3.6 %collective-permute-start = (bf16[3,16,704]{2,1,0:T(8,128)(2,1)S(1)}, bf16[3,16,704]{2,1,0:T(8,128)(2,1)S(1)}, u32[]{:S(2)}, u32[]{:S(2)}) collective-permute-start(bf16[3,16,704]{2,1,0:T(8,128)(2,1)S(1)} %get-tuple-element.90), channel_id=1, source_target_pairs={{0,8},{8,16},{16,24},{1,9},{9,17},{17,25},{2,10},{10,18},{18,26},{... | collective-permute-start | bytes 202760 | tf_op jit(solution)/shard_map/ppermute | solution.py:17
  12.5 2.4 %collective-permute-start.1 = (bf16[3,16,704]{2,1,0:T(8,128)(2,1)S(1)}, bf16[3,16,704]{2,1,0:T(8,128)(2,1)S(1)}, u32[]{:S(2)}, u32[]{:S(2)}) collective-permute-start(bf16[3,16,704]{2,1,0:T(8,128)(2,1)S(1)} %get-tuple-element.89), channel_id=1, source_target_pairs={{8,0},{16,8},{24,16},{9,1},{17,9},{25,17},{10,2},{18,10},{26,18},{... | collective-permute-start | bytes 202760 | tf_op jit(solution)/shard_map/ppermute | solution.py:20
  14.9 0.8 copy.27
  15.9 1.3 reduce_sum.166
  17.3 0.7 broadcast_compare_fusion.1
  17.9 0.8 select_reduce_fusion.8
  28.8 2.7 %add_convert_fusion.4 = f32[4]{0:T(128)S(1)} fusion(s32[1]{0:T(128)} %bitcast.3, s32[1]{0:T(128)} %bitcast.2, s32[1]{0:T(128)} %bitcast.1, s32[1]{0:T(128)} %bitcast), kind=kLoop, calls=%fused_computation.313 | loop fusion | flops 16 | bytes 32 | tf_op jit(solution)/shard_map/convert_element_type | solution.py:107
  32.4 1.9 collective-permute-start.2
  34.3 3.6 %collective-permute-start.3 = (bf16[30,3,704]{2,1,0:T(4,128)(2,1)S(1)}, bf16[30,3,704]{2,1,0:T(4,128)(2,1)S(1)}, u32[]{:S(2)}, u32[]{:S(2)}) collective-permute-start(bf16[30,3,704]{2,1,0:T(4,128)(2,1)S(1)} %get-tuple-element.86), channel_id=1, source_target_pairs={{2,0},{4,2},{6,4},{3,1},{5,3},{7,5},{10,8},{12,10},{14,12},{11,9},... | collective-permute-start | bytes 380168 | tf_op jit(solution)/shard_map/ppermute | solution.py:20
  38.1 1.1 collective-permute-done.2
  39.2 1.8 collective-permute-done.3
  41.0 0.6 pad_maximum_fusion.1
  41.6 0.7 dynamic-slice_bitcast_fusion.3
  43.0 5.8 %add_convert_fusion.2 = bf16[4,8,8,704]{3,2,1,0:T(8,128)(2,1)S(1)} fusion(bf16[4,14,14,704]{3,2,1,0:T(8,128)(2,1)S(1)} %pad_maximum_fusion, f32[704]{0:T(1024)S(1)} %copy-done.4, f32[704]{0:T(1024)S(1)} %get-tuple-element.53, f32[704]{0:T(1024)S(1)} %get-tuple-element.54, f32[704]{0:T(1024)S(1)} %get-tuple-element.7, f32[704]{0:T(1024)S(1)} %get-tuple-element.8, ...), kind=kLoop, calls=%fused_computation.138 | loop fusion | flops 26673152 | bytes 18163200 | tf_op jit(solution)/shard_map/convert_element_type | solution.py:144
  48.8 1.6 collective-permute-start.4
  51.1 0.6 fusion.95
  51.8 9.1 %collective-permute-done.4 = bf16[256,704]{1,0:T(8,128)(2,1)S(1)} collective-permute-done((bf16[256,704]{1,0:T(8,128)(2,1)S(1)}, bf16[256,704]{1,0:T(8,128)(2,1)S(1)}, u32[]{:S(2)}, u32[]{:S(2)}) %collective-permute-start.4) | collective-permute-done | bytes 360480 | tf_op jit(solution)/shard_map/ppermute | solution.py:57
  61.5 0.7 fusion.15
  62.2 7.7 %convolution_add_fusion = f32[256,2816]{1,0:T(8,128)} fusion(bf16[1408,2816]{1,0:T(8,128)(2,1)} %param.18, f32[2816]{0:T(1024)S(1)} %copy-done.6, f32[1408]{0:T(1024)S(1)} %copy-done.8, f32[1408]{0:T(1024)S(1)} %copy-done.9, f32[256]{0:T(256)S(1)} %add_rsqrt_fusion, f32[256]{0:T(256)S(1)} %broadcast_multiply_fusion, bf16[256,704]{1,0:T(8,128)(2,1)S(1)} %bitcast.70, ...), kind=kOutput, calls=%fused_computation.47 | convolution fusion | flops 2036170752 | bytes 11558913 | tf_op jit(solution)/shard_map/dot_general | solution.py:151
  69.9 12.2 %all-gather.2.cloned.1.call-done = bf16[1408,2816]{1,0:T(8,128)(2,1)} async-done(((bf16[88,2816]{1,0:T(8,128)(2,1)}), bf16[1408,2816]{1,0:T(8,128)(2,1)}) %all-gather.2.cloned.1.call-update) | async-done | bytes 7929872 | tf_op jit(solution)/shard_map/all_gather | solution.py:99
  82.0 8.3 %fusion.10 = (f32[2816]{0:T(1024)S(1)}, f32[2816]{0:T(1024)S(1)}, bf16[256,2816]{1,0:T(8,128)(2,1)}, f32[256,2816]{1,0:T(8,128)}) fusion(f32[256]{0:T(256)S(1)} %convert_element_type.365, f32[256,2816]{1,0:T(8,128)} %convolution_add_fusion, bf16[1408,2816]{1,0:T(8,128)(2,1)} %all-gather.2.cloned.1.call-done, ...), kind=kOutput, calls=%fused_computation.58 | convolution fusion | flops 2041211392 | bytes 15883265 | tf_op jit(solution)/shard_map/dot_general | solution.py:159
  90.3 48.0 %all-reduce.2 = (f32[2816]{0:T(1024)S(1)}, f32[2816]{0:T(1024)S(1)}) all-reduce(f32[2816]{0:T(1024)S(1)} %get-tuple-element.4, f32[2816]{0:T(1024)S(1)} %get-tuple-element.5), channel_id=1, replica_groups=mesh['sy'=4,'sx'=4,'tp'=2] {'sy','sx'}, use_global_device_ids=true, to_apply=%region_16.17 | all-reduce | flops 5632 | bytes 45056 | tf_op jit(solution)/shard_map/psum | solution.py:61
  138.3 0.7 multiply_reduce_fusion.1
  139.7 1.4 collective-permute-start.5
  141.1 0.7 fusion.106
  153.5 0.7 broadcast_in_dim.17
  154.2 0.7 collective-permute-start.8
  154.9 0.6 broadcast_add_fusion.1
  156.7 1.1 collective-permute-done.8
  157.8 0.7 broadcast_add_fusion
  159.8 6.3 %fusion.16 = f32[256,1408]{1,0:T(8,128)S(1)} fusion(bf16[1408,2816]{1,0:T(8,128)(2,1)} %all-gather.2.cloned.1.call-done, bf16[256,2816]{1,0:T(8,128)(2,1)} %get-tuple-element.69, f32[2816]{0:T(1024)S(1)} %copy-done.7, f32[2816]{0:T(1024)S(1)} %get-tuple-element.68, f32[2816]{0:T(1024)S(1)} %copy-done.3), kind=kOutput, calls=%fused_computation.109 | convolution fusion | flops 2034368512 | bytes 10847232 | tf_op jit(solution)/shard_map/dot_general | solution.py:164
  166.2 0.7 collective-permute-start.6
  167.0 6.9 %fusion.102 = (f32[256]{0:T(256)S(1)}, f32[256]{0:T(256)S(1)}, f32[256,1408]{1,0:T(8,128)S(1)}, f32[256,1408]{1,0:T(8,128)S(1)}) fusion(f32[256]{0:T(256)S(1)} %add_rsqrt_fusion, f32[256]{0:T(256)S(1)} %broadcast_multiply_fusion, bf16[256,704]{1,0:T(8,128)(2,1)S(1)} %bitcast.71, bf16[256,704]{1,0:T(8,128)(2,1)S(1)} %collective-permute-done.4, ...), kind=kOutput, calls=%fused_computation.322 | convolution fusion | flops 2047344128 | bytes 18787840 | tf_op jit(solution)/shard_map/dot_general | solution.py:179
  173.9 1.4 collective-permute-start.10
  175.5 0.7 collective-permute-start.9
  176.2 1.4 collective-permute-done.10
  177.7 5.7 %collective-permute-done.9 = bf16[256,704]{1,0:T(8,128)(2,1)S(1)} collective-permute-done((bf16[256,704]{1,0:T(8,128)(2,1)S(1)}, bf16[256,704]{1,0:T(8,128)(2,1)S(1)}, u32[]{:S(2)}, u32[]{:S(2)}) %collective-permute-start.9) | collective-permute-done | bytes 360480 | tf_op jit(solution)/shard_map/ppermute | solution.py:57
  183.4 0.9 multiply_convert_fusion.1
  184.5 10.4 %collective-permute-start.12 = (bf16[3,16,704]{2,1,0:T(8,128)(2,1)S(1)}, bf16[3,16,704]{2,1,0:T(8,128)(2,1)S(1)}, u32[]{:S(2)}, u32[]{:S(2)}) collective-permute-start(bf16[3,16,704]{2,1,0:T(8,128)(2,1)S(1)} %fusion.93), channel_id=1, source_target_pairs={{8,0},{16,8},{24,16},{9,1},{17,9},{25,17},{10,2},{18,10},{26,18},{... | collective-permute-start | bytes 202760 | tf_op jit(solution)/shard_map/ppermute | solution.py:20
  194.9 1.9 collective-permute-start.11
  197.0 1.0 fusion.28
  197.9 3.2 %collective-permute-done.11 = bf16[3,16,704]{2,1,0:T(8,128)(2,1)S(1)} collective-permute-done((bf16[3,16,704]{2,1,0:T(8,128)(2,1)S(1)}, bf16[3,16,704]{2,1,0:T(8,128)(2,1)S(1)}, u32[]{:S(2)}, u32[]{:S(2)}) %collective-permute-start.11) | collective-permute-done | bytes 67616 | tf_op jit(solution)/shard_map/ppermute | solution.py:17
  201.4 1.9 collective-permute-start.13
  203.3 2.4 %collective-permute-start.14 = (bf16[30,3,704]{2,1,0:T(4,128)(2,1)S(1)}, bf16[30,3,704]{2,1,0:T(4,128)(2,1)S(1)}, u32[]{:S(2)}, u32[]{:S(2)}) collective-permute-start(bf16[30,3,704]{2,1,0:T(4,128)(2,1)S(1)} %get-tuple-element.84), channel_id=1, source_target_pairs={{0,2},{2,4},{4,6},{1,3},{3,5},{5,7},{8,10},{10,12},{12,14},{9,11},... | collective-permute-start | bytes 380168 | tf_op jit(solution)/shard_map/ppermute | solution.py:17
  206.4 7.1 %collective-permute-done.14 = bf16[30,3,704]{2,1,0:T(4,128)(2,1)S(1)} collective-permute-done((bf16[30,3,704]{2,1,0:T(4,128)(2,1)S(1)}, bf16[30,3,704]{2,1,0:T(4,128)(2,1)S(1)}, u32[]{:S(2)}, u32[]{:S(2)}) %collective-permute-start.14) | collective-permute-done | bytes 126752 | tf_op jit(solution)/shard_map/ppermute | solution.py:17
  213.5 14.9 %add_convert_fusion.1 = bf16[24,16,704]{2,1,0:T(8,128)(2,1)} fusion(bf16[24,16,704]{2,1,0:T(8,128)(2,1)S(1)} %copy-done.1, bf16[30,16,704]{2,1,0:T(8,128)(2,1)S(1)} %constant_dynamic-update-slice_fusion.3, bf16[30,3,704]{2,1,0:T(4,128)(2,1)S(1)} %collective-permute-done.14, bf16[30,3,704]{2,1,0:T(4,128)(2,1)S(1)} %collective-permute-done.13, ...), kind=kLoop, calls=%fused_computation.130 | loop fusion | flops 77316096 | bytes 5933312 | tf_op jit(solution)/shard_map/convert_element_type | solution.py:196
  (75 shorter events, 6.4 us)
Async XLA Ops:
  7.2 24.6 %copy-start.1 = (bf16[24,16,704]{2,1,0:T(8,128)(2,1)S(1)}, bf16[24,16,704]{2,1,0:T(8,128)(2,1)}, u32[]{:S(2)}) copy-start(bf16[24,16,704]{2,1,0:T(8,128)(2,1)} %param.25) | copy-start | bytes 1622020
  7.2 74.8 %all-gather.2.cloned.1.call-start = ((), (), s32[]{:S(2)}) async-start(), calls=%async_computation | async-start | bytes 8425472 | tf_op jit(solution)/shard_map/all_gather | solution.py:99
  7.9 23.9 %copy-start.2 = (f32[7,7,704]{2,1,0:T(8,128)S(1)}, f32[7,7,704]{2,1,0:T(8,128)}, u32[]{:S(2)}) copy-start(f32[7,7,704]{2,1,0:T(8,128)} %param.14) | copy-start | bytes 413956
  8.9 23.2 %copy-start = (bf16[24,16,704]{2,1,0:T(8,128)(2,1)S(1)}, bf16[24,16,704]{2,1,0:T(8,128)(2,1)}, u32[]{:S(2)}) copy-start(bf16[24,16,704]{2,1,0:T(8,128)(2,1)} %param.13) | copy-start | bytes 1622020
  8.9 23.2 %collective-permute-start = (bf16[3,16,704]{2,1,0:T(8,128)(2,1)S(1)}, bf16[3,16,704]{2,1,0:T(8,128)(2,1)S(1)}, u32[]{:S(2)}, u32[]{:S(2)}) collective-permute-start(bf16[3,16,704]{2,1,0:T(8,128)(2,1)S(1)} %get-tuple-element.90), channel_id=1, source_target_pairs={{0,8},{8,16},{16,24},{1,9},{9,17},{17,25},{2,10},{10,18},{18,26},{... | collective-permute-start | bytes 202760 | tf_op jit(solution)/shard_map/ppermute | solution.py:17
  12.5 19.7 %collective-permute-start.1 = (bf16[3,16,704]{2,1,0:T(8,128)(2,1)S(1)}, bf16[3,16,704]{2,1,0:T(8,128)(2,1)S(1)}, u32[]{:S(2)}, u32[]{:S(2)}) collective-permute-start(bf16[3,16,704]{2,1,0:T(8,128)(2,1)S(1)} %get-tuple-element.89), channel_id=1, source_target_pairs={{8,0},{16,8},{24,16},{9,1},{17,9},{25,17},{10,2},{18,10},{26,18},{... | collective-permute-start | bytes 202760 | tf_op jit(solution)/shard_map/ppermute | solution.py:20
  32.4 6.9 %collective-permute-start.2 = (bf16[30,3,704]{2,1,0:T(4,128)(2,1)S(1)}, bf16[30,3,704]{2,1,0:T(4,128)(2,1)S(1)}, u32[]{:S(2)}, u32[]{:S(2)}) collective-permute-start(bf16[30,3,704]{2,1,0:T(4,128)(2,1)S(1)} %get-tuple-element.85), channel_id=1, source_target_pairs={{0,2},{2,4},{4,6},{1,3},{3,5},{5,7},{8,10},{10,12},{12,14},{9,11},... | collective-permute-start | bytes 380168 | tf_op jit(solution)/shard_map/ppermute | solution.py:17
  34.3 6.7 %collective-permute-start.3 = (bf16[30,3,704]{2,1,0:T(4,128)(2,1)S(1)}, bf16[30,3,704]{2,1,0:T(4,128)(2,1)S(1)}, u32[]{:S(2)}, u32[]{:S(2)}) collective-permute-start(bf16[30,3,704]{2,1,0:T(4,128)(2,1)S(1)} %get-tuple-element.86), channel_id=1, source_target_pairs={{2,0},{4,2},{6,4},{3,1},{5,3},{7,5},{10,8},{12,10},{14,12},{11,9},... | collective-permute-start | bytes 380168 | tf_op jit(solution)/shard_map/ppermute | solution.py:20
  42.3 0.7 copy-start.4
  48.8 13.4 %copy-start.6 = (f32[2816]{0:T(1024)S(1)}, f32[2816]{0:T(1024)}, u32[]{:S(2)}) copy-start(f32[2816]{0:T(1024)} %param.19) | copy-start | bytes 33796
  48.8 13.4 %copy-start.8 = (f32[1408]{0:T(1024)S(1)}, f32[1408]{0:T(1024)}, u32[]{:S(2)}) copy-start(f32[1408]{0:T(1024)} %param.17) | copy-start | bytes 16900
  48.8 13.4 %copy-start.9 = (f32[1408]{0:T(1024)S(1)}, f32[1408]{0:T(1024)}, u32[]{:S(2)}) copy-start(f32[1408]{0:T(1024)} %param.16) | copy-start | bytes 16900
  48.8 12.1 %collective-permute-start.4 = (bf16[256,704]{1,0:T(8,128)(2,1)S(1)}, bf16[256,704]{1,0:T(8,128)(2,1)S(1)}, u32[]{:S(2)}, u32[]{:S(2)}) collective-permute-start(bf16[256,704]{1,0:T(8,128)(2,1)S(1)} %bitcast.67), channel_id=1, source_target_pairs={{0,1},{1,0},{2,3},{3,2},{4,5},{5,4},{6,7},{7,6},{8,9},{9,8},{10,11... | collective-permute-start | bytes 1081352 | tf_op jit(solution)/shard_map/ppermute | solution.py:57
  50.5 19.3 %collective-permute-start.7 = (bf16[256,704]{1,0:T(8,128)(2,1)S(1)}, bf16[256,704]{1,0:T(8,128)(2,1)S(1)}, u32[]{:S(2)}, u32[]{:S(2)}) collective-permute-start(bf16[256,704]{1,0:T(8,128)(2,1)S(1)} %fusion.29), channel_id=1, source_target_pairs={{0,1},{1,0},{2,3},{3,2},{4,5},{5,4},{6,7},{7,6},{8,9},{9,8},{10,11... | collective-permute-start | bytes 1081352 | tf_op jit(solution)/shard_map/ppermute | solution.py:57
  69.9 68.5 %copy-start.3 = (f32[2816]{0:T(1024)S(1)}, f32[2816]{0:T(1024)}, u32[]{:S(2)}) copy-start(f32[2816]{0:T(1024)} %param.20) | copy-start | bytes 33796
  69.9 89.9 %copy-start.7 = (f32[2816]{0:T(1024)S(1)}, f32[2816]{0:T(1024)}, u32[]{:S(2)}) copy-start(f32[2816]{0:T(1024)} %param.21) | copy-start | bytes 33796
  139.7 15.2 %collective-permute-start.5 = (f32[8,128]{1,0:T(8,128)S(1)}, f32[8,128]{1,0:T(8,128)S(1)}, u32[]{:S(2)}, u32[]{:S(2)}) collective-permute-start(f32[8,128]{1,0:T(8,128)S(1)} %broadcast_in_dim.16), channel_id=1, source_target_pairs={{0,1},{1,0},{2,3},{3,2},{4,5},{5,4},{6,7},{7,6},{8,9},{9,8},{10,11... | collective-permute-start | bytes 12296 | tf_op jit(solution)/shard_map/ppermute | solution.py:57
  154.2 3.7 %collective-permute-start.8 = (f32[8,128]{1,0:T(8,128)S(1)}, f32[8,128]{1,0:T(8,128)S(1)}, u32[]{:S(2)}, u32[]{:S(2)}) collective-permute-start(f32[8,128]{1,0:T(8,128)S(1)} %broadcast_in_dim.17), channel_id=1, source_target_pairs={{0,1},{1,0},{2,3},{3,2},{4,5},{5,4},{6,7},{7,6},{8,9},{9,8},{10,11... | collective-permute-start | bytes 12296 | tf_op jit(solution)/shard_map/ppermute | solution.py:57
  159.7 7.2 %copy-start.10 = (f32[256,2816]{1,0:T(8,128)S(1)}, f32[256,2816]{1,0:T(8,128)}, u32[]{:S(2)}) copy-start(f32[256,2816]{1,0:T(8,128)} %convolution_add_fusion) | copy-start | bytes 8650756
  159.8 7.2 %copy-start.11 = (f32[256,2816]{1,0:T(8,128)S(1)}, f32[256,2816]{1,0:T(8,128)}, u32[]{:S(2)}) copy-start(f32[256,2816]{1,0:T(8,128)} %get-tuple-element.114) | copy-start | bytes 8650756
  159.8 7.2 %copy-start.12 = (bf16[256,2816]{1,0:T(8,128)(2,1)S(1)}, bf16[256,2816]{1,0:T(8,128)(2,1)}, u32[]{:S(2)}) copy-start(bf16[256,2816]{1,0:T(8,128)(2,1)} %get-tuple-element.69) | copy-start | bytes 4325380
  166.2 11.4 %collective-permute-start.6 = (bf16[256,704]{1,0:T(8,128)(2,1)S(1)}, bf16[256,704]{1,0:T(8,128)(2,1)S(1)}, u32[]{:S(2)}, u32[]{:S(2)}) collective-permute-start(bf16[256,704]{1,0:T(8,128)(2,1)S(1)} %dynamic-slice_convert_fusion.1), channel_id=1, source_target_pairs={{0,1},{1,0},{2,3},{3,2},{4,5},{5,4},{6,7},{7,6},{8,9},{9,8},{10,11... | collective-permute-start | bytes 1081352 | tf_op jit(solution)/shard_map/ppermute | solution.py:57
  167.0 16.4 %copy-start.5 = (f32[704]{0:T(1024)S(1)}, f32[704]{0:T(1024)}, u32[]{:S(2)}) copy-start(f32[704]{0:T(1024)} %param.23) | copy-start | bytes 8452
  173.9 3.7 %collective-permute-start.10 = (f32[2,256]{1,0:T(2,128)S(1)}, f32[2,256]{1,0:T(2,128)S(1)}, u32[]{:S(2)}, u32[]{:S(2)}) collective-permute-start(f32[2,256]{1,0:T(2,128)S(1)} %pad_maximum_fusion.8), channel_id=1, source_target_pairs={{0,1},{1,0},{2,3},{3,2},{4,5},{5,4},{6,7},{7,6},{8,9},{9,8},{10,11... | collective-permute-start | bytes 6152 | tf_op jit(solution)/shard_map/ppermute | solution.py:57
  175.5 7.8 %collective-permute-start.9 = (bf16[256,704]{1,0:T(8,128)(2,1)S(1)}, bf16[256,704]{1,0:T(8,128)(2,1)S(1)}, u32[]{:S(2)}, u32[]{:S(2)}) collective-permute-start(bf16[256,704]{1,0:T(8,128)(2,1)S(1)} %dynamic-slice_convert_fusion), channel_id=1, source_target_pairs={{0,1},{1,0},{2,3},{3,2},{4,5},{5,4},{6,7},{7,6},{8,9},{9,8},{10,11... | collective-permute-start | bytes 1081352 | tf_op jit(solution)/shard_map/ppermute | solution.py:57
  184.5 16.8 %collective-permute-start.12 = (bf16[3,16,704]{2,1,0:T(8,128)(2,1)S(1)}, bf16[3,16,704]{2,1,0:T(8,128)(2,1)S(1)}, u32[]{:S(2)}, u32[]{:S(2)}) collective-permute-start(bf16[3,16,704]{2,1,0:T(8,128)(2,1)S(1)} %fusion.93), channel_id=1, source_target_pairs={{8,0},{16,8},{24,16},{9,1},{17,9},{25,17},{10,2},{18,10},{26,18},{... | collective-permute-start | bytes 202760 | tf_op jit(solution)/shard_map/ppermute | solution.py:20
  194.9 6.2 %collective-permute-start.11 = (bf16[3,16,704]{2,1,0:T(8,128)(2,1)S(1)}, bf16[3,16,704]{2,1,0:T(8,128)(2,1)S(1)}, u32[]{:S(2)}, u32[]{:S(2)}) collective-permute-start(bf16[3,16,704]{2,1,0:T(8,128)(2,1)S(1)} %fusion.94), channel_id=1, source_target_pairs={{0,8},{8,16},{16,24},{1,9},{9,17},{17,25},{2,10},{10,18},{18,26},{... | collective-permute-start | bytes 202760 | tf_op jit(solution)/shard_map/ppermute | solution.py:17
  201.4 5.0 %collective-permute-start.13 = (bf16[30,3,704]{2,1,0:T(4,128)(2,1)S(1)}, bf16[30,3,704]{2,1,0:T(4,128)(2,1)S(1)}, u32[]{:S(2)}, u32[]{:S(2)}) collective-permute-start(bf16[30,3,704]{2,1,0:T(4,128)(2,1)S(1)} %get-tuple-element.83), channel_id=1, source_target_pairs={{2,0},{4,2},{6,4},{3,1},{5,3},{7,5},{10,8},{12,10},{14,12},{11,9},... | collective-permute-start | bytes 380168 | tf_op jit(solution)/shard_map/ppermute | solution.py:20
  203.3 10.2 %collective-permute-start.14 = (bf16[30,3,704]{2,1,0:T(4,128)(2,1)S(1)}, bf16[30,3,704]{2,1,0:T(4,128)(2,1)S(1)}, u32[]{:S(2)}, u32[]{:S(2)}) collective-permute-start(bf16[30,3,704]{2,1,0:T(4,128)(2,1)S(1)} %get-tuple-element.84), channel_id=1, source_target_pairs={{0,2},{2,4},{4,6},{1,3},{3,5},{5,7},{8,10},{10,12},{12,14},{9,11},... | collective-permute-start | bytes 380168 | tf_op jit(solution)/shard_map/ppermute | solution.py:17
Sparse Core Ops, SparseCore 0:
  10.2 71.7 all-gather.1
where the time goes:
time: 236 us; the launch traced here: 235 us
  blocking collectives  48 us (20%)
  waiting for transfers between devices  43.9 us (19%)
  between operations  37.6 us (16%)
  starting transfers between devices  35.4 us (15%)
  other arithmetic  33.5 us (14%)
  matrix products  29.1 us (12%)
  local copies, waits for them, and re-layouts  7.66 us (3%)
    psum x1, blocking collectives, over_pixels(): return lax.psum(vector, ('sy', 'sx'))  48 us
    ppermute x4, starting transfers between devices, extended(): lax.ppermute(lax.slice_in_dim(block, 0, width, axis=dim), axis, backward)  18.3 us
    ppermute x7, waiting for transfers between devices, swapped(): return lax.ppermute(array, 'tp', [(i, count - 1 - i) for i in range(count)])  17.4 us
    convert_element_type x1, other arithmetic, shards(): feature_grad = (cotangent.astype(jnp.float32) + depthwise(extend(grad_ima...  14.9 us
    all_gather x1, waiting for transfers between devices, shards(): down_t = lax.all_gather(down_weight.T, ('sy', 'sx'), axis=0, tiled=True)  12.2 us
    ppermute x4, waiting for transfers between devices, extended(): lax.ppermute(lax.slice_in_dim(block, block.shape[dim] - width, None, axis...  11.4 us
    ppermute x4, starting transfers between devices, extended(): lax.ppermute(lax.slice_in_dim(block, block.shape[dim] - width, None, axis...  9.87 us
    dot_general x1, matrix products, shards(): back_hidden = jnp.dot(cot_wide, down_t, preferred_element_type=jnp.float32)  8.27 us
  transfers between devices with their start and end apart: 16, of which 10 were waited for; matrix products, arithmetic and copies ran while one was open for 15% of the time, Pallas kernels for 0%

commit v1 on v0

--- a/solution.py
+++ b/solution.py
@@ -58,7 +58,7 @@
 
 
 def over_pixels(vector):
-    return lax.psum(vector, ("sy", "sx"))
+    return lax.psum(lax.psum(vector, "sx"), "sy")
 
 
 def conv_tiles(windows, kernel):

time: 236 us -> 206 us (0.87)
  blocking collectives: 48 us -> 26.1 us
  starting transfers between devices: 35.4 us -> 30.3 us
  waiting for transfers between devices: 43.9 us -> 40.8 us
    psum x1 -> x2, blocking collectives: 48 us -> 26.1 us  [over_pixels(): return lax.psum(lax.psum(vector, 'sx'), 'sy')]
    ppermute x4, starting transfers between devices: 18.3 us -> 13.3 us  [extended(): lax.ppermute(lax.slice_in_dim(block, 0, width, axis=dim), axis, backward)]
    ppermute x4, waiting for transfers between devices: 11.4 us -> 8.13 us  [extended(): lax.ppermute(lax.slice_in_dim(block, block.shape[dim] - width, None, axis...]
  transfers between devices with their start and end apart: 16 -> 16, of which waited for: 10 -> 10; matrix products, arithmetic and copies ran while one was open for 15% -> 18% of each run, Pallas kernels for 0% -> 0%
where the time goes in v1:
time: 206 us; the launch traced here: 205 us
  waiting for transfers between devices  40.8 us (20%)
  between operations  37.6 us (18%)
  other arithmetic  33.4 us (16%)
  starting transfers between devices  30.3 us (15%)
  matrix products  29.1 us (14%)
  blocking collectives  26.1 us (13%)
  local copies, waits for them, and re-layouts  7.67 us (4%)
    psum x2, blocking collectives, over_pixels(): return lax.psum(lax.psum(vector, 'sx'), 'sy')  26.1 us
    ppermute x7, waiting for transfers between devices, swapped(): return lax.ppermute(array, 'tp', [(i, count - 1 - i) for i in range(count)])  17.5 us
    convert_element_type x1, other arithmetic, shards(): feature_grad = (cotangent.astype(jnp.float32) + depthwise(extend(grad_ima...  14.9 us
    ppermute x4, starting transfers between devices, extended(): lax.ppermute(lax.slice_in_dim(block, 0, width, axis=dim), axis, backward)  13.3 us
    all_gather x1, waiting for transfers between devices, shards(): down_t = lax.all_gather(down_weight.T, ('sy', 'sx'), axis=0, tiled=True)  12.1 us
    ppermute x4, starting transfers between devices, extended(): lax.ppermute(lax.slice_in_dim(block, block.shape[dim] - width, None, axis...  9.87 us
    dot_general x1, matrix products, shards(): back_hidden = jnp.dot(cot_wide, down_t, preferred_element_type=jnp.float32)  8.26 us
    ppermute x4, waiting for transfers between devices, extended(): lax.ppermute(lax.slice_in_dim(block, block.shape[dim] - width, None, axis...  8.13 us
  transfers between devices with their start and end apart: 16, of which 10 were waited for; matrix products, arithmetic and copies ran while one was open for 18% of the time, Pallas kernels for 0%

profile of v1, /device:TPU:12, one launch (start us, length us, event | category | flops | bytes accessed | tf_op | source)
XLA Modules:
  0.0 205.0 jit_solution(6884685768434847341)
XLA Ops:
  7.2 0.7 all-gather.2.cloned.1.call-update
  7.9 1.0 fusion.105
  8.9 3.6 %collective-permute-start = (bf16[3,16,704]{2,1,0:T(8,128)(2,1)S(1)}, bf16[3,16,704]{2,1,0:T(8,128)(2,1)S(1)}, u32[]{:S(2)}, u32[]{:S(2)}) collective-permute-start(bf16[3,16,704]{2,1,0:T(8,128)(2,1)S(1)} %get-tuple-element.92), channel_id=1, source_target_pairs={{0,8},{8,16},{16,24},{1,9},{9,17},{17,25},{2,10},{10,18},{18,26},{... | collective-permute-start | bytes 202760 | tf_op jit(solution)/shard_map/ppermute | solution.py:17
  12.5 2.4 %collective-permute-start.1 = (bf16[3,16,704]{2,1,0:T(8,128)(2,1)S(1)}, bf16[3,16,704]{2,1,0:T(8,128)(2,1)S(1)}, u32[]{:S(2)}, u32[]{:S(2)}) collective-permute-start(bf16[3,16,704]{2,1,0:T(8,128)(2,1)S(1)} %get-tuple-element.91), channel_id=1, source_target_pairs={{8,0},{16,8},{24,16},{9,1},{17,9},{25,17},{10,2},{18,10},{26,18},{... | collective-permute-start | bytes 202760 | tf_op jit(solution)/shard_map/ppermute | solution.py:20
  14.9 0.8 copy.27
  15.9 1.3 reduce_sum.166
  17.3 0.7 broadcast_compare_fusion.1
  17.9 0.8 select_reduce_fusion.8
  28.8 2.7 %add_convert_fusion.4 = f32[4]{0:T(128)S(1)} fusion(s32[1]{0:T(128)} %bitcast.3, s32[1]{0:T(128)} %bitcast.2, s32[1]{0:T(128)} %bitcast.1, s32[1]{0:T(128)} %bitcast), kind=kLoop, calls=%fused_computation.313 | loop fusion | flops 16 | bytes 32 | tf_op jit(solution)/shard_map/convert_element_type | solution.py:107
  32.4 1.9 collective-permute-start.2
  34.3 3.6 %collective-permute-start.3 = (bf16[30,3,704]{2,1,0:T(4,128)(2,1)S(1)}, bf16[30,3,704]{2,1,0:T(4,128)(2,1)S(1)}, u32[]{:S(2)}, u32[]{:S(2)}) collective-permute-start(bf16[30,3,704]{2,1,0:T(4,128)(2,1)S(1)} %get-tuple-element.88), channel_id=1, source_target_pairs={{2,0},{4,2},{6,4},{3,1},{5,3},{7,5},{10,8},{12,10},{14,12},{11,9},... | collective-permute-start | bytes 380168 | tf_op jit(solution)/shard_map/ppermute | solution.py:20
  38.1 1.1 collective-permute-done.2
  39.2 1.8 collective-permute-done.3
  41.0 0.6 pad_maximum_fusion.1
  41.6 0.7 dynamic-slice_bitcast_fusion.3
  43.0 5.8 %add_convert_fusion.2 = bf16[4,8,8,704]{3,2,1,0:T(8,128)(2,1)S(1)} fusion(bf16[4,14,14,704]{3,2,1,0:T(8,128)(2,1)S(1)} %pad_maximum_fusion, f32[704]{0:T(1024)S(1)} %copy-done.4, f32[704]{0:T(1024)S(1)} %get-tuple-element.53, f32[704]{0:T(1024)S(1)} %get-tuple-element.54, f32[704]{0:T(1024)S(1)} %get-tuple-element.7, f32[704]{0:T(1024)S(1)} %get-tuple-element.8, ...), kind=kLoop, calls=%fused_computation.138 | loop fusion | flops 26673152 | bytes 18163200 | tf_op jit(solution)/shard_map/convert_element_type | solution.py:144
  48.8 1.6 collective-permute-start.4
  51.1 0.6 fusion.95
  51.8 9.1 %collective-permute-done.4 = bf16[256,704]{1,0:T(8,128)(2,1)S(1)} collective-permute-done((bf16[256,704]{1,0:T(8,128)(2,1)S(1)}, bf16[256,704]{1,0:T(8,128)(2,1)S(1)}, u32[]{:S(2)}, u32[]{:S(2)}) %collective-permute-start.4) | collective-permute-done | bytes 360480 | tf_op jit(solution)/shard_map/ppermute | solution.py:57
  61.5 0.7 fusion.15
  62.2 7.7 %convolution_add_fusion = f32[256,2816]{1,0:T(8,128)} fusion(bf16[1408,2816]{1,0:T(8,128)(2,1)} %param.18, f32[2816]{0:T(1024)S(1)} %copy-done.6, f32[1408]{0:T(1024)S(1)} %copy-done.8, f32[1408]{0:T(1024)S(1)} %copy-done.9, f32[256]{0:T(256)S(1)} %add_rsqrt_fusion, f32[256]{0:T(256)S(1)} %broadcast_multiply_fusion, bf16[256,704]{1,0:T(8,128)(2,1)S(1)} %bitcast.70, ...), kind=kOutput, calls=%fused_computation.47 | convolution fusion | flops 2036170752 | bytes 11558913 | tf_op jit(solution)/shard_map/dot_general | solution.py:151
  69.9 12.1 %all-gather.2.cloned.1.call-done = bf16[1408,2816]{1,0:T(8,128)(2,1)} async-done(((bf16[88,2816]{1,0:T(8,128)(2,1)}), bf16[1408,2816]{1,0:T(8,128)(2,1)}) %all-gather.2.cloned.1.call-update) | async-done | bytes 7929872 | tf_op jit(solution)/shard_map/all_gather | solution.py:99
  82.0 8.3 %fusion.10 = (f32[2816]{0:T(1024)S(1)}, f32[2816]{0:T(1024)S(1)}, bf16[256,2816]{1,0:T(8,128)(2,1)}, f32[256,2816]{1,0:T(8,128)}) fusion(f32[256]{0:T(256)S(1)} %convert_element_type.365, f32[256,2816]{1,0:T(8,128)} %convolution_add_fusion, bf16[1408,2816]{1,0:T(8,128)(2,1)} %all-gather.2.cloned.1.call-done, ...), kind=kOutput, calls=%fused_computation.58 | convolution fusion | flops 2041211392 | bytes 15883265 | tf_op jit(solution)/shard_map/dot_general | solution.py:159
  90.3 11.4 %all-reduce.2 = (f32[2816]{0:T(1024)S(1)}, f32[2816]{0:T(1024)S(1)}) all-reduce(f32[2816]{0:T(1024)S(1)} %get-tuple-element.4, f32[2816]{0:T(1024)S(1)} %get-tuple-element.5), channel_id=1, replica_groups=mesh['sy'=4,'sx'=4,'tp'=2] {'sx'}, use_global_device_ids=true, to_apply=%region_17.18 | all-reduce | flops 5632 | bytes 45056 | tf_op jit(solution)/shard_map/psum | solution.py:61
  101.7 14.7 %all-reduce.3 = (f32[2816]{0:T(1024)S(1)}, f32[2816]{0:T(1024)S(1)}) all-reduce(f32[2816]{0:T(1024)S(1)} %get-tuple-element.65, f32[2816]{0:T(1024)S(1)} %get-tuple-element.66), channel_id=1, replica_groups=mesh['sy'=4,'sx'=4,'tp'=2] {'sy'}, use_global_device_ids=true, to_apply=%region_18.19 | all-reduce | flops 5632 | bytes 45056 | tf_op jit(solution)/shard_map/psum | solution.py:61
  116.4 0.7 multiply_reduce_fusion.1
  117.1 0.6 broadcast_in_dim.16
  117.7 1.5 collective-permute-start.5
  119.3 0.7 fusion.106
  131.6 0.7 broadcast_in_dim.17
  133.0 0.6 broadcast_add_fusion.1
  134.8 1.2 collective-permute-done.8
  136.0 0.7 broadcast_add_fusion
  137.9 6.3 %fusion.16 = f32[256,1408]{1,0:T(8,128)S(1)} fusion(bf16[1408,2816]{1,0:T(8,128)(2,1)} %all-gather.2.cloned.1.call-done, bf16[256,2816]{1,0:T(8,128)(2,1)} %get-tuple-element.71, f32[2816]{0:T(1024)S(1)} %copy-done.7, f32[2816]{0:T(1024)S(1)} %get-tuple-element.70, f32[2816]{0:T(1024)S(1)} %copy-done.3), kind=kOutput, calls=%fused_computation.109 | convolution fusion | flops 2034368512 | bytes 10847232 | tf_op jit(solution)/shard_map/dot_general | solution.py:164
  145.0 6.9 %fusion.102 = (f32[256]{0:T(256)S(1)}, f32[256]{0:T(256)S(1)}, f32[256,1408]{1,0:T(8,128)S(1)}, f32[256,1408]{1,0:T(8,128)S(1)}) fusion(f32[256]{0:T(256)S(1)} %add_rsqrt_fusion, f32[256]{0:T(256)S(1)} %broadcast_multiply_fusion, bf16[256,704]{1,0:T(8,128)(2,1)S(1)} %bitcast.71, bf16[256,704]{1,0:T(8,128)(2,1)S(1)} %collective-permute-done.4, ...), kind=kOutput, calls=%fused_computation.322 | convolution fusion | flops 2047344128 | bytes 18787840 | tf_op jit(solution)/shard_map/dot_general | solution.py:179
  151.9 1.5 collective-permute-start.10
  153.6 0.6 collective-permute-start.9
  154.3 1.4 collective-permute-done.10
  155.7 5.8 %collective-permute-done.9 = bf16[256,704]{1,0:T(8,128)(2,1)S(1)} collective-permute-done((bf16[256,704]{1,0:T(8,128)(2,1)S(1)}, bf16[256,704]{1,0:T(8,128)(2,1)S(1)}, u32[]{:S(2)}, u32[]{:S(2)}) %collective-permute-start.9) | collective-permute-done | bytes 360480 | tf_op jit(solution)/shard_map/ppermute | solution.py:57
  161.5 0.9 multiply_convert_fusion.1
  162.5 5.4 %collective-permute-start.12 = (bf16[3,16,704]{2,1,0:T(8,128)(2,1)S(1)}, bf16[3,16,704]{2,1,0:T(8,128)(2,1)S(1)}, u32[]{:S(2)}, u32[]{:S(2)}) collective-permute-start(bf16[3,16,704]{2,1,0:T(8,128)(2,1)S(1)} %fusion.93), channel_id=1, source_target_pairs={{8,0},{16,8},{24,16},{9,1},{17,9},{25,17},{10,2},{18,10},{26,18},{... | collective-permute-start | bytes 202760 | tf_op jit(solution)/shard_map/ppermute | solution.py:20
  168.0 1.9 collective-permute-start.11
  170.1 1.0 fusion.28
  171.0 3.2 %collective-permute-done.11 = bf16[3,16,704]{2,1,0:T(8,128)(2,1)S(1)} collective-permute-done((bf16[3,16,704]{2,1,0:T(8,128)(2,1)S(1)}, bf16[3,16,704]{2,1,0:T(8,128)(2,1)S(1)}, u32[]{:S(2)}, u32[]{:S(2)}) %collective-permute-start.11) | collective-permute-done | bytes 67616 | tf_op jit(solution)/shard_map/ppermute | solution.py:17
  174.5 1.9 collective-permute-start.13
  176.4 2.4 %collective-permute-start.14 = (bf16[30,3,704]{2,1,0:T(4,128)(2,1)S(1)}, bf16[30,3,704]{2,1,0:T(4,128)(2,1)S(1)}, u32[]{:S(2)}, u32[]{:S(2)}) collective-permute-start(bf16[30,3,704]{2,1,0:T(4,128)(2,1)S(1)} %get-tuple-element.86), channel_id=1, source_target_pairs={{0,2},{2,4},{4,6},{1,3},{3,5},{5,7},{8,10},{10,12},{12,14},{9,11},... | collective-permute-start | bytes 380168 | tf_op jit(solution)/shard_map/ppermute | solution.py:17
  179.5 3.8 %collective-permute-done.14 = bf16[30,3,704]{2,1,0:T(4,128)(2,1)S(1)} collective-permute-done((bf16[30,3,704]{2,1,0:T(4,128)(2,1)S(1)}, bf16[30,3,704]{2,1,0:T(4,128)(2,1)S(1)}, u32[]{:S(2)}, u32[]{:S(2)}) %collective-permute-start.14) | collective-permute-done | bytes 126752 | tf_op jit(solution)/shard_map/ppermute | solution.py:17
  183.3 14.9 %add_convert_fusion.1 = bf16[24,16,704]{2,1,0:T(8,128)(2,1)} fusion(bf16[24,16,704]{2,1,0:T(8,128)(2,1)S(1)} %copy-done.1, bf16[30,16,704]{2,1,0:T(8,128)(2,1)S(1)} %constant_dynamic-update-slice_fusion.3, bf16[30,3,704]{2,1,0:T(4,128)(2,1)S(1)} %collective-permute-done.14, bf16[30,3,704]{2,1,0:T(4,128)(2,1)S(1)} %collective-permute-done.13, ...), kind=kLoop, calls=%fused_computation.130 | loop fusion | flops 77316096 | bytes 5933312 | tf_op jit(solution)/shard_map/convert_element_type | solution.py:196
  (76 shorter events, 7.1 us)
Async XLA Ops:
  7.2 24.6 %copy-start.1 = (bf16[24,16,704]{2,1,0:T(8,128)(2,1)S(1)}, bf16[24,16,704]{2,1,0:T(8,128)(2,1)}, u32[]{:S(2)}) copy-start(bf16[24,16,704]{2,1,0:T(8,128)(2,1)} %param.25) | copy-start | bytes 1622020
  7.2 74.8 %all-gather.2.cloned.1.call-start = ((), (), s32[]{:S(2)}) async-start(), calls=%async_computation | async-start | bytes 8425472 | tf_op jit(solution)/shard_map/all_gather | solution.py:99
  7.9 23.9 %copy-start.2 = (f32[7,7,704]{2,1,0:T(8,128)S(1)}, f32[7,7,704]{2,1,0:T(8,128)}, u32[]{:S(2)}) copy-start(f32[7,7,704]{2,1,0:T(8,128)} %param.14) | copy-start | bytes 413956
  8.9 23.2 %copy-start = (bf16[24,16,704]{2,1,0:T(8,128)(2,1)S(1)}, bf16[24,16,704]{2,1,0:T(8,128)(2,1)}, u32[]{:S(2)}) copy-start(bf16[24,16,704]{2,1,0:T(8,128)(2,1)} %param.13) | copy-start | bytes 1622020
  8.9 23.2 %collective-permute-start = (bf16[3,16,704]{2,1,0:T(8,128)(2,1)S(1)}, bf16[3,16,704]{2,1,0:T(8,128)(2,1)S(1)}, u32[]{:S(2)}, u32[]{:S(2)}) collective-permute-start(bf16[3,16,704]{2,1,0:T(8,128)(2,1)S(1)} %get-tuple-element.92), channel_id=1, source_target_pairs={{0,8},{8,16},{16,24},{1,9},{9,17},{17,25},{2,10},{10,18},{18,26},{... | collective-permute-start | bytes 202760 | tf_op jit(solution)/shard_map/ppermute | solution.py:17
  12.5 19.7 %collective-permute-start.1 = (bf16[3,16,704]{2,1,0:T(8,128)(2,1)S(1)}, bf16[3,16,704]{2,1,0:T(8,128)(2,1)S(1)}, u32[]{:S(2)}, u32[]{:S(2)}) collective-permute-start(bf16[3,16,704]{2,1,0:T(8,128)(2,1)S(1)} %get-tuple-element.91), channel_id=1, source_target_pairs={{8,0},{16,8},{24,16},{9,1},{17,9},{25,17},{10,2},{18,10},{26,18},{... | collective-permute-start | bytes 202760 | tf_op jit(solution)/shard_map/ppermute | solution.py:20
  32.4 6.9 %collective-permute-start.2 = (bf16[30,3,704]{2,1,0:T(4,128)(2,1)S(1)}, bf16[30,3,704]{2,1,0:T(4,128)(2,1)S(1)}, u32[]{:S(2)}, u32[]{:S(2)}) collective-permute-start(bf16[30,3,704]{2,1,0:T(4,128)(2,1)S(1)} %get-tuple-element.87), channel_id=1, source_target_pairs={{0,2},{2,4},{4,6},{1,3},{3,5},{5,7},{8,10},{10,12},{12,14},{9,11},... | collective-permute-start | bytes 380168 | tf_op jit(solution)/shard_map/ppermute | solution.py:17
  34.3 6.7 %collective-permute-start.3 = (bf16[30,3,704]{2,1,0:T(4,128)(2,1)S(1)}, bf16[30,3,704]{2,1,0:T(4,128)(2,1)S(1)}, u32[]{:S(2)}, u32[]{:S(2)}) collective-permute-start(bf16[30,3,704]{2,1,0:T(4,128)(2,1)S(1)} %get-tuple-element.88), channel_id=1, source_target_pairs={{2,0},{4,2},{6,4},{3,1},{5,3},{7,5},{10,8},{12,10},{14,12},{11,9},... | collective-permute-start | bytes 380168 | tf_op jit(solution)/shard_map/ppermute | solution.py:20
  42.3 0.7 copy-start.4
  48.8 13.4 %copy-start.6 = (f32[2816]{0:T(1024)S(1)}, f32[2816]{0:T(1024)}, u32[]{:S(2)}) copy-start(f32[2816]{0:T(1024)} %param.19) | copy-start | bytes 33796
  48.8 13.4 %copy-start.8 = (f32[1408]{0:T(1024)S(1)}, f32[1408]{0:T(1024)}, u32[]{:S(2)}) copy-start(f32[1408]{0:T(1024)} %param.17) | copy-start | bytes 16900
  48.8 13.4 %copy-start.9 = (f32[1408]{0:T(1024)S(1)}, f32[1408]{0:T(1024)}, u32[]{:S(2)}) copy-start(f32[1408]{0:T(1024)} %param.16) | copy-start | bytes 16900
  48.8 12.1 %collective-permute-start.4 = (bf16[256,704]{1,0:T(8,128)(2,1)S(1)}, bf16[256,704]{1,0:T(8,128)(2,1)S(1)}, u32[]{:S(2)}, u32[]{:S(2)}) collective-permute-start(bf16[256,704]{1,0:T(8,128)(2,1)S(1)} %bitcast.67), channel_id=1, source_target_pairs={{0,1},{1,0},{2,3},{3,2},{4,5},{5,4},{6,7},{7,6},{8,9},{9,8},{10,11... | collective-permute-start | bytes 1081352 | tf_op jit(solution)/shard_map/ppermute | solution.py:57
  50.5 19.3 %collective-permute-start.7 = (bf16[256,704]{1,0:T(8,128)(2,1)S(1)}, bf16[256,704]{1,0:T(8,128)(2,1)S(1)}, u32[]{:S(2)}, u32[]{:S(2)}) collective-permute-start(bf16[256,704]{1,0:T(8,128)(2,1)S(1)} %fusion.29), channel_id=1, source_target_pairs={{0,1},{1,0},{2,3},{3,2},{4,5},{5,4},{6,7},{7,6},{8,9},{9,8},{10,11... | collective-permute-start | bytes 1081352 | tf_op jit(solution)/shard_map/ppermute | solution.py:57
  69.9 46.5 %copy-start.3 = (f32[2816]{0:T(1024)S(1)}, f32[2816]{0:T(1024)}, u32[]{:S(2)}) copy-start(f32[2816]{0:T(1024)} %param.20) | copy-start | bytes 33796
  69.9 68.0 %copy-start.7 = (f32[2816]{0:T(1024)S(1)}, f32[2816]{0:T(1024)}, u32[]{:S(2)}) copy-start(f32[2816]{0:T(1024)} %param.21) | copy-start | bytes 33796
  117.7 15.2 %collective-permute-start.5 = (f32[8,128]{1,0:T(8,128)S(1)}, f32[8,128]{1,0:T(8,128)S(1)}, u32[]{:S(2)}, u32[]{:S(2)}) collective-permute-start(f32[8,128]{1,0:T(8,128)S(1)} %broadcast_in_dim.16), channel_id=1, source_target_pairs={{0,1},{1,0},{2,3},{3,2},{4,5},{5,4},{6,7},{7,6},{8,9},{9,8},{10,11... | collective-permute-start | bytes 12296 | tf_op jit(solution)/shard_map/ppermute | solution.py:57
  132.3 3.7 %collective-permute-start.8 = (f32[8,128]{1,0:T(8,128)S(1)}, f32[8,128]{1,0:T(8,128)S(1)}, u32[]{:S(2)}, u32[]{:S(2)}) collective-permute-start(f32[8,128]{1,0:T(8,128)S(1)} %broadcast_in_dim.17), channel_id=1, source_target_pairs={{0,1},{1,0},{2,3},{3,2},{4,5},{5,4},{6,7},{7,6},{8,9},{9,8},{10,11... | collective-permute-start | bytes 12296 | tf_op jit(solution)/shard_map/ppermute | solution.py:57
  137.9 7.1 %copy-start.10 = (f32[256,2816]{1,0:T(8,128)S(1)}, f32[256,2816]{1,0:T(8,128)}, u32[]{:S(2)}) copy-start(f32[256,2816]{1,0:T(8,128)} %convolution_add_fusion) | copy-start | bytes 8650756
  137.9 7.1 %copy-start.11 = (f32[256,2816]{1,0:T(8,128)S(1)}, f32[256,2816]{1,0:T(8,128)}, u32[]{:S(2)}) copy-start(f32[256,2816]{1,0:T(8,128)} %get-tuple-element.116) | copy-start | bytes 8650756
  137.9 7.1 %copy-start.12 = (bf16[256,2816]{1,0:T(8,128)(2,1)S(1)}, bf16[256,2816]{1,0:T(8,128)(2,1)}, u32[]{:S(2)}) copy-start(bf16[256,2816]{1,0:T(8,128)(2,1)} %get-tuple-element.71) | copy-start | bytes 4325380
  144.4 11.3 %collective-permute-start.6 = (bf16[256,704]{1,0:T(8,128)(2,1)S(1)}, bf16[256,704]{1,0:T(8,128)(2,1)S(1)}, u32[]{:S(2)}, u32[]{:S(2)}) collective-permute-start(bf16[256,704]{1,0:T(8,128)(2,1)S(1)} %dynamic-slice_convert_fusion.1), channel_id=1, source_target_pairs={{0,1},{1,0},{2,3},{3,2},{4,5},{5,4},{6,7},{7,6},{8,9},{9,8},{10,11... | collective-permute-start | bytes 1081352 | tf_op jit(solution)/shard_map/ppermute | solution.py:57
  145.0 16.4 %copy-start.5 = (f32[704]{0:T(1024)S(1)}, f32[704]{0:T(1024)}, u32[]{:S(2)}) copy-start(f32[704]{0:T(1024)} %param.23) | copy-start | bytes 8452
  151.9 3.7 %collective-permute-start.10 = (f32[2,256]{1,0:T(2,128)S(1)}, f32[2,256]{1,0:T(2,128)S(1)}, u32[]{:S(2)}, u32[]{:S(2)}) collective-permute-start(f32[2,256]{1,0:T(2,128)S(1)} %pad_maximum_fusion.8), channel_id=1, source_target_pairs={{0,1},{1,0},{2,3},{3,2},{4,5},{5,4},{6,7},{7,6},{8,9},{9,8},{10,11... | collective-permute-start | bytes 6152 | tf_op jit(solution)/shard_map/ppermute | solution.py:57
  153.6 7.8 %collective-permute-start.9 = (bf16[256,704]{1,0:T(8,128)(2,1)S(1)}, bf16[256,704]{1,0:T(8,128)(2,1)S(1)}, u32[]{:S(2)}, u32[]{:S(2)}) collective-permute-start(bf16[256,704]{1,0:T(8,128)(2,1)S(1)} %dynamic-slice_convert_fusion), channel_id=1, source_target_pairs={{0,1},{1,0},{2,3},{3,2},{4,5},{5,4},{6,7},{7,6},{8,9},{9,8},{10,11... | collective-permute-start | bytes 1081352 | tf_op jit(solution)/shard_map/ppermute | solution.py:57
  162.5 11.8 %collective-permute-start.12 = (bf16[3,16,704]{2,1,0:T(8,128)(2,1)S(1)}, bf16[3,16,704]{2,1,0:T(8,128)(2,1)S(1)}, u32[]{:S(2)}, u32[]{:S(2)}) collective-permute-start(bf16[3,16,704]{2,1,0:T(8,128)(2,1)S(1)} %fusion.93), channel_id=1, source_target_pairs={{8,0},{16,8},{24,16},{9,1},{17,9},{25,17},{10,2},{18,10},{26,18},{... | collective-permute-start | bytes 202760 | tf_op jit(solution)/shard_map/ppermute | solution.py:20
  168.0 6.2 %collective-permute-start.11 = (bf16[3,16,704]{2,1,0:T(8,128)(2,1)S(1)}, bf16[3,16,704]{2,1,0:T(8,128)(2,1)S(1)}, u32[]{:S(2)}, u32[]{:S(2)}) collective-permute-start(bf16[3,16,704]{2,1,0:T(8,128)(2,1)S(1)} %fusion.94), channel_id=1, source_target_pairs={{0,8},{8,16},{16,24},{1,9},{9,17},{17,25},{2,10},{10,18},{18,26},{... | collective-permute-start | bytes 202760 | tf_op jit(solution)/shard_map/ppermute | solution.py:17
  174.5 5.0 %collective-permute-start.13 = (bf16[30,3,704]{2,1,0:T(4,128)(2,1)S(1)}, bf16[30,3,704]{2,1,0:T(4,128)(2,1)S(1)}, u32[]{:S(2)}, u32[]{:S(2)}) collective-permute-start(bf16[30,3,704]{2,1,0:T(4,128)(2,1)S(1)} %get-tuple-element.85), channel_id=1, source_target_pairs={{2,0},{4,2},{6,4},{3,1},{5,3},{7,5},{10,8},{12,10},{14,12},{11,9},... | collective-permute-start | bytes 380168 | tf_op jit(solution)/shard_map/ppermute | solution.py:20
  176.4 6.9 %collective-permute-start.14 = (bf16[30,3,704]{2,1,0:T(4,128)(2,1)S(1)}, bf16[30,3,704]{2,1,0:T(4,128)(2,1)S(1)}, u32[]{:S(2)}, u32[]{:S(2)}) collective-permute-start(bf16[30,3,704]{2,1,0:T(4,128)(2,1)S(1)} %get-tuple-element.86), channel_id=1, source_target_pairs={{0,2},{2,4},{4,6},{1,3},{3,5},{5,7},{8,10},{10,12},{12,14},{9,11},... | collective-permute-start | bytes 380168 | tf_op jit(solution)/shard_map/ppermute | solution.py:17
Sparse Core Ops, SparseCore 0:
  10.2 71.7 all-gather.1
